TPU v7x, 32 devices: a whole 2x2x4 slice. The times are simulated.
32 devices in a mesh: group: 2 (over x), tm: 16 (over z, y, core).
Axes of the slice: x: 2, y: 2, z: 4, core: 2. Of those that a mesh axis runs over, the one named last changes fastest.
Arguments:
- patches: bfloat16 [32, 1024, 128], P(('group', 'tm')), parts along dimension 0, may hold values from -6 to 6
- classes: int32 [32], P(('group', 'tm')), parts along dimension 0, may hold values from 0 to 15
- dilations: int32 [4], replicated, may hold values from 1 to 4, as said below
- enc_weight: bfloat16 [128, 256], replicated, may hold values from -0.5 to 0.5
- cond_table: bfloat16 [16, 256], replicated, may hold values from -3 to 3
- temp_weight: bfloat16 [4, 512, 256], replicated, may hold values from -0.25 to 0.25
- dec_weight: bfloat16 [256, 128], replicated, may hold values from -0.375 to 0.375
- cotangent: bfloat16 [32, 1024, 128], P(('group', 'tm')), parts along dimension 0, may hold values from -0.125 to 0.125
Outputs:
- decoded: bfloat16 [32, 1024, 128], P(('group', 'tm')), parts along dimension 0
- grad_encoder: float32 [256, 256], P(('group', 'tm')), parts along dimension 0
- grad_temporal: float32 [8, 512, 256], P('group', 'tm'), parts along dimension 0
- grad_decoder: float32 [512, 128], P(('group', 'tm')), parts along dimension 0
There are 2 independent parts, one for each index of `group`. A program takes and returns all parts, laid end to end along the dimension named above; an argument that names none is the same for every part. Nothing has to cross between parts.
Inputs may be any that keep to these rules, and one draw needn't show every extreme that they name: `dilations`: every layer's dilation lies in 1 to 4, and some layer's is exactly 4.
All inputs are finite; a program needn't handle non-finite values.
Results may differ from a plain program's by a relative error of at most 0.009.
Values may be sent and summed in bfloat16 or wider, within the bound.
A program may use at most 64 MiB of HBM per device.

v0:
```python
import jax
import jax.numpy as jnp
from jax import lax
from jax.sharding import PartitionSpec as P


def shift_late(values, spacing, margin):
    filler = jnp.zeros((margin,) + values.shape[1:], values.dtype)
    padded = jnp.concatenate([filler, values], axis=0)
    return lax.dynamic_slice_in_dim(padded, margin - spacing, values.shape[0], 0)


def shift_early(values, spacing, margin):
    filler = jnp.zeros((margin,) + values.shape[1:], values.dtype)
    padded = jnp.concatenate([values, filler], axis=0)
    return lax.dynamic_slice_in_dim(padded, spacing, values.shape[0], 0)


def encode_rows(patch_rows, frame_kinds, enc_weight, cond_table):
    kinds = cond_table.shape[0]
    onehot = (frame_kinds[:, None] == jnp.arange(kinds, dtype=jnp.int32)[None, :]).astype(
        jnp.bfloat16
    )
    embedded = jnp.dot(onehot, cond_table, preferred_element_type=jnp.float32)
    start = jnp.einsum("tpc,cd->tpd", patch_rows, enc_weight, preferred_element_type=jnp.float32)
    return (start + embedded[:, None, :]).astype(jnp.bfloat16)


def shards(patches, classes, dilations, enc_weight, cond_table, temp_weight, dec_weight, cotangent):
    layers = temp_weight.shape[0]
    width = temp_weight.shape[2]
    start = encode_rows(patches, classes, enc_weight, cond_table)
    latent = lax.all_to_all(start, "tm", split_axis=1, concat_axis=0, tiled=True)
    margin = latent.shape[0] // 4
    saved = []
    for layer in range(layers):
        joined = jnp.concatenate([latent, shift_late(latent, dilations[layer], margin)], axis=-1)
        pre_act = jnp.einsum(
            "tpk,kd->tpd", joined, temp_weight[layer], preferred_element_type=jnp.float32
        )
        saved.append((joined, pre_act))
        latent = (latent.astype(jnp.float32) + jax.nn.silu(pre_act)).astype(jnp.bfloat16)
    final = lax.all_to_all(latent, "tm", split_axis=0, concat_axis=1, tiled=True)
    decoded = jnp.einsum(
        "fpd,dc->fpc", final, dec_weight, preferred_element_type=jnp.float32
    ).astype(jnp.bfloat16)
    dec_term = jnp.einsum("fpd,fpc->dc", final, cotangent, preferred_element_type=jnp.float32)
    upstream = jnp.einsum(
        "fpc,dc->fpd", cotangent, dec_weight, preferred_element_type=jnp.float32
    ).astype(jnp.bfloat16)
    carried = lax.all_to_all(upstream, "tm", split_axis=1, concat_axis=0, tiled=True)
    layer_terms = [None] * layers
    for layer in reversed(range(layers)):
        joined, pre_act = saved[layer]
        gate_value = jax.nn.sigmoid(pre_act)
        dpre = (
            carried.astype(jnp.float32) * gate_value * (1.0 + pre_act * (1.0 - gate_value))
        ).astype(jnp.bfloat16)
        layer_term = jnp.einsum("tpk,tpd->kd", joined, dpre, preferred_element_type=jnp.float32)
        layer_terms[layer] = layer_term
        returned = jnp.einsum(
            "tpd,kd->tpk", dpre, temp_weight[layer], preferred_element_type=jnp.float32
        )
        carried = (
            carried.astype(jnp.float32)
            + returned[..., :width]
            + shift_early(returned[..., width:], dilations[layer], margin)
        ).astype(jnp.bfloat16)
    stacked = jnp.stack(layer_terms)
    grad_temporal = lax.psum_scatter(stacked, "tm", scatter_dimension=1, tiled=True)
    carried_frames = lax.all_to_all(carried, "tm", split_axis=0, concat_axis=1, tiled=True)
    enc_term = jnp.einsum(
        "fpc,fpd->cd", patches, carried_frames, preferred_element_type=jnp.float32
    )
    grad_encoder, grad_decoder = (
        lax.psum_scatter(enc_term, "tm", scatter_dimension=0, tiled=True),
        lax.psum_scatter(dec_term, "tm", scatter_dimension=0, tiled=True),
    )
    return (decoded, grad_encoder, grad_temporal, grad_decoder)


def solution(mesh):
    in_specs = (
        P(("group", "tm"), None, None),
        P(("group", "tm")),
        P(),
        P(),
        P(),
        P(),
        P(),
        P(("group", "tm"), None, None),
    )
    out_specs = (
        P(("group", "tm"), None, None),
        P(("group", "tm"), None),
        P("group", "tm", None),
        P(("group", "tm"), None),
    )
    return jax.shard_map(shards, mesh=mesh, in_specs=in_specs, out_specs=out_specs, check_vma=False)
```

profile of v0, /device:TPU:0, one launch (start us, length us, event | category | flops | bytes accessed | tf_op | source)
XLA Modules:
  0.0 280.7 jit_solution(17788033939454266709)
XLA Ops:
  7.9 0.8 fusion.47
  8.7 1.2 fusion.2
  9.9 0.8 copy.26
  11.3 3.8 %reduce.1 = bf16[1024,256]{1,0:T(8,128)(2,1)S(1)} reduce(bf16[1024,1,256]{2,1,0:T(2,128)(2,1)S(1)} %bitcast.97, bf16[]{:T(256)} %broadcast.31), dimensions={1}, to_apply=%bitcast.92.reduce_sub_computation | reduce | bytes 1048578
  15.1 0.9 reshape.78
  16.0 7.4 %all-to-all-start = ((bf16[16,2,8192]{2,1,0:T(2,128)(2,1)}), bf16[16,2,8192]{2,1,0:T(2,128)(2,1)S(1)}, u32[]{:S(2)}, u32[]{:S(2)}) async-start(bf16[16,2,8192]{2,1,0:T(2,128)(2,1)} %reshape.78), calls=%async_computation | async-start | bytes 1048576 | tf_op jit(solution)/shard_map/all_to_all | solution.py:33
  24.6 3.8 %reduce = bf16[1024,256]{1,0:T(8,128)(2,1)S(1)} reduce(bf16[1024,1,256]{2,1,0:T(2,128)(2,1)S(1)} %bitcast.98, bf16[]{:T(256)} %broadcast.31), dimensions={1}, to_apply=%bitcast.91.reduce_sub_computation | reduce | bytes 1048578
  28.4 0.9 reshape.76
  29.4 8.5 %all-to-all-done = bf16[16,2,8192]{2,1,0:T(2,128)(2,1)S(1)} async-done(((bf16[16,2,8192]{2,1,0:T(2,128)(2,1)}), bf16[16,2,8192]{2,1,0:T(2,128)(2,1)S(1)}, u32[]{:S(2)}, u32[]{:S(2)}) %all-to-all-start) | async-done | bytes 524320 | tf_op jit(solution)/shard_map/all_to_all | solution.py:33
  37.9 4.1 %all-to-all-start.2 = ((bf16[16,2,8192]{2,1,0:T(2,128)(2,1)}), bf16[16,2,8192]{2,1,0:T(2,128)(2,1)S(1)}, u32[]{:S(2)}, u32[]{:S(2)}) async-start(bf16[16,2,8192]{2,1,0:T(2,128)(2,1)} %reshape.76), calls=%async_computation.2 | async-start | bytes 1048576 | tf_op jit(solution)/shard_map/all_to_all | solution.py:51
  57.2 2.6 add_convert_fusion.3
  59.9 1.4 add_convert_fusion.2
  61.4 1.4 add_convert_fusion.1
  62.9 1.5 multiply_convert_fusion
  64.4 5.7 %all-to-all-start.1 = ((bf16[16,64,256]{2,1,0:T(8,128)(2,1)}), bf16[16,64,256]{2,1,0:T(8,128)(2,1)S(1)}, u32[]{:S(2)}, u32[]{:S(2)}) async-start(bf16[16,64,256]{2,1,0:T(8,128)(2,1)} %get-tuple-element.17), calls=%async_computation.1 | async-start | bytes 1048576 | tf_op jit(solution)/shard_map/all_to_all | solution.py:43
  70.1 1.4 fusion.25
  72.0 0.9 copy-done.19
  74.2 0.9 copy-done.23
  76.2 0.9 copy-done.21
  77.9 1.1 fusion.11
  79.1 1.5 convolution_bitcast_fusion.1
  80.6 4.0 %all-to-all-done.1 = bf16[16,64,256]{2,1,0:T(8,128)(2,1)S(1)} async-done(((bf16[16,64,256]{2,1,0:T(8,128)(2,1)}), bf16[16,64,256]{2,1,0:T(8,128)(2,1)S(1)}, u32[]{:S(2)}, u32[]{:S(2)}) %all-to-all-start.1) | async-done | bytes 524320 | tf_op jit(solution)/shard_map/all_to_all | solution.py:43
  84.6 4.1 %all-to-all-start.3 = ((bf16[16,64,256]{2,1,0:T(8,128)(2,1)}), bf16[16,64,256]{2,1,0:T(8,128)(2,1)S(1)}, u32[]{:S(2)}, u32[]{:S(2)}) async-start(bf16[16,64,256]{2,1,0:T(8,128)(2,1)} %fusion.11), calls=%async_computation.3 | async-start | bytes 1048576 | tf_op jit(solution)/shard_map/all_to_all | solution.py:71
  88.8 3.1 %convolution_bitcast_fusion.2 = f32[1,512,256]{2,1,0:T(8,128)} fusion(bf16[16,64,256]{2,1,0:T(8,128)(2,1)} %copy-done.7, bf16[16,64,256]{2,1,0:T(8,128)(2,1)} %copy-done.6, bf16[16,64,256]{2,1,0:T(8,128)(2,1)S(1)} %fusion.7, f32[16,64,256]{2,1,0:T(8,128)} %get-tuple-element.25), kind=kOutput, calls=%fused_computation.18 | convolution fusion | flops 273154048 | bytes 3145728 | tf_op jit(solution)/shard_map/tpk,tpd->kd/dot_general | solution.py:59
  91.9 1.5 convolution_bitcast_fusion.3
  93.4 1.0 fusion.22
  94.5 8.7 %all-to-all-done.3 = bf16[16,64,256]{2,1,0:T(8,128)(2,1)S(1)} async-done(((bf16[16,64,256]{2,1,0:T(8,128)(2,1)}), bf16[16,64,256]{2,1,0:T(8,128)(2,1)S(1)}, u32[]{:S(2)}, u32[]{:S(2)}) %all-to-all-start.3) | async-done | bytes 524320 | tf_op jit(solution)/shard_map/all_to_all | solution.py:71
  105.7 1.5 pad_maximum_fusion
  107.2 1.0 fusion.3
  108.2 42.8 %reduce-scatter.8.cloned.1.call-done = f32[16,128]{1,0:T(8,128)} async-done(((f32[256,128]{1,0:T(8,128)}), f32[16,128]{1,0:T(8,128)}) %reduce-scatter.8.cloned.1.call-update) | async-done | bytes 8208 | tf_op jit(solution)/shard_map/reduce_scatter | solution.py:77
  151.0 58.2 %reduce-scatter.10.cloned.1.call-done = f32[8,256]{1,0:T(8,128)} async-done(((f32[128,256]{1,0:T(8,128)}), f32[8,256]{1,0:T(8,128)}) %reduce-scatter.10.cloned.1.call-update) | async-done | bytes 8208
  209.2 65.0 %reduce-scatter.6.cloned.1.call-done = f32[4,32,256]{2,1,0:T(8,128)} async-done(((f32[4,512,256]{2,1,0:T(8,128)}), f32[4,32,256]{2,1,0:T(8,128)}) %reduce-scatter.6.cloned.1.call-update) | async-done | bytes 131088 | tf_op jit(solution)/shard_map/reduce_scatter | solution.py:70
  (79 shorter events, 10.2 us)
Async XLA Ops:
  7.2 16.3 %copy-start = (bf16[1,1024,128]{2,1,0:T(8,128)(2,1)S(1)}, bf16[1,1024,128]{2,1,0:T(8,128)(2,1)}, u32[]{:S(2)}) copy-start(bf16[1,1024,128]{2,1,0:T(8,128)(2,1)} %param.15) | copy-start | bytes 786436
  10.7 12.7 %copy-start.17 = (bf16[256,128]{1,0:T(8,128)(2,1)S(1)}, bf16[256,128]{1,0:T(8,128)(2,1)}, u32[]{:S(2)}) copy-start(bf16[256,128]{1,0:T(8,128)(2,1)} %param.14) | copy-start | bytes 196612
  16.0 21.9 %all-to-all-start = ((bf16[16,2,8192]{2,1,0:T(2,128)(2,1)}), bf16[16,2,8192]{2,1,0:T(2,128)(2,1)S(1)}, u32[]{:S(2)}, u32[]{:S(2)}) async-start(bf16[16,2,8192]{2,1,0:T(2,128)(2,1)} %reshape.78), calls=%async_computation | async-start | bytes 1048576 | tf_op jit(solution)/shard_map/all_to_all | solution.py:33
  24.6 17.4 %copy-start.20 = (s32[4]{0:T(128)S(1)}, s32[4]{0:T(128)}, u32[]{:S(2)}) copy-start(s32[4]{0:T(128)} %param.10) | copy-start | bytes 52
  37.9 18.6 %all-to-all-start.2 = ((bf16[16,2,8192]{2,1,0:T(2,128)(2,1)}), bf16[16,2,8192]{2,1,0:T(2,128)(2,1)S(1)}, u32[]{:S(2)}, u32[]{:S(2)}) async-start(bf16[16,2,8192]{2,1,0:T(2,128)(2,1)} %reshape.76), calls=%async_computation.2 | async-start | bytes 1048576 | tf_op jit(solution)/shard_map/all_to_all | solution.py:51
  57.2 2.6 copy-start.4
  57.2 2.7 copy-start.18
  59.8 3.0 %copy-start.6 = (bf16[16,64,256]{2,1,0:T(8,128)(2,1)}, bf16[16,64,256]{2,1,0:T(8,128)(2,1)S(1)}, u32[]{:S(2)}) copy-start(bf16[16,64,256]{2,1,0:T(8,128)(2,1)S(1)} %get-tuple-element.22) | copy-start | bytes 1572868
  59.9 3.0 %copy-start.7 = (bf16[16,64,256]{2,1,0:T(8,128)(2,1)}, bf16[16,64,256]{2,1,0:T(8,128)(2,1)S(1)}, u32[]{:S(2)}) copy-start(bf16[16,64,256]{2,1,0:T(8,128)(2,1)S(1)} %pad_dynamic-slice_fusion.6) | copy-start | bytes 1572868
  61.3 1.5 copy-start.8
  61.4 1.5 copy-start.10
  62.9 1.5 copy-start.2
  64.4 7.2 %copy-start.12 = (bf16[16,64,256]{2,1,0:T(8,128)(2,1)}, bf16[16,64,256]{2,1,0:T(8,128)(2,1)S(1)}, u32[]{:S(2)}) copy-start(bf16[16,64,256]{2,1,0:T(8,128)(2,1)S(1)} %get-tuple-element.16) | copy-start | bytes 1572868
  64.4 20.2 %all-to-all-start.1 = ((bf16[16,64,256]{2,1,0:T(8,128)(2,1)}), bf16[16,64,256]{2,1,0:T(8,128)(2,1)S(1)}, u32[]{:S(2)}, u32[]{:S(2)}) async-start(bf16[16,64,256]{2,1,0:T(8,128)(2,1)} %get-tuple-element.17), calls=%async_computation.1 | async-start | bytes 1048576 | tf_op jit(solution)/shard_map/all_to_all | solution.py:43
  71.7 1.2 copy-start.19
  71.7 1.5 copy-start.24
  74.0 1.2 copy-start.23
  75.9 1.2 copy-start.21
  77.9 1.1 copy-start.9
  77.9 1.2 copy-start.11
  84.6 18.6 %all-to-all-start.3 = ((bf16[16,64,256]{2,1,0:T(8,128)(2,1)}), bf16[16,64,256]{2,1,0:T(8,128)(2,1)S(1)}, u32[]{:S(2)}, u32[]{:S(2)}) async-start(bf16[16,64,256]{2,1,0:T(8,128)(2,1)} %fusion.11), calls=%async_computation.3 | async-start | bytes 1048576 | tf_op jit(solution)/shard_map/all_to_all | solution.py:71
  88.7 62.3 %reduce-scatter.8.cloned.1.call-start = ((), (), s32[]{:S(2)}) async-start(), calls=%async_computation.8 | async-start | bytes 139264 | tf_op jit(solution)/shard_map/reduce_scatter | solution.py:77
  88.8 3.2 %copy-start.5 = (bf16[16,64,256]{2,1,0:T(8,128)(2,1)S(1)}, bf16[16,64,256]{2,1,0:T(8,128)(2,1)}, u32[]{:S(2)}) copy-start(bf16[16,64,256]{2,1,0:T(8,128)(2,1)} %copy-done.4) | copy-start | bytes 1572868
  88.8 3.2 %copy-start.22 = (f32[16,64,256]{2,1,0:T(8,128)S(1)}, f32[16,64,256]{2,1,0:T(8,128)}, u32[]{:S(2)}) copy-start(f32[16,64,256]{2,1,0:T(8,128)} %get-tuple-element.23) | copy-start | bytes 3145732
  91.9 11.2 %copy-start.1 = (bf16[1,1024,128]{2,1,0:T(8,128)(2,1)S(1)}, bf16[1,1024,128]{2,1,0:T(8,128)(2,1)}, u32[]{:S(2)}) copy-start(bf16[1,1024,128]{2,1,0:T(8,128)(2,1)} %param.8) | copy-start | bytes 786436
  93.4 10.9 %copy-start.3 = (bf16[16,64,256]{2,1,0:T(8,128)(2,1)S(1)}, bf16[16,64,256]{2,1,0:T(8,128)(2,1)}, u32[]{:S(2)}) copy-start(bf16[16,64,256]{2,1,0:T(8,128)(2,1)} %copy-done.2) | copy-start | bytes 1572868
  93.4 10.9 %copy-start.13 = (bf16[16,64,256]{2,1,0:T(8,128)(2,1)S(1)}, bf16[16,64,256]{2,1,0:T(8,128)(2,1)}, u32[]{:S(2)}) copy-start(bf16[16,64,256]{2,1,0:T(8,128)(2,1)} %copy-done.12) | copy-start | bytes 1572868
  94.5 114.7 %reduce-scatter.10.cloned.1.call-start = ((), (), s32[]{:S(2)}) async-start(), calls=%async_computation.9 | async-start | bytes 139264
  104.3 1.0 copy-start.14
  104.3 169.9 %reduce-scatter.6.cloned.1.call-start = ((), (), s32[]{:S(2)}) async-start(), calls=%async_computation.7 | async-start | bytes 2228224 | tf_op jit(solution)/shard_map/reduce_scatter | solution.py:70
  104.4 1.1 copy-start.15
  104.4 1.3 copy-start.16
Sparse Core Ops, SparseCore 0:
  94.6 56.3 reduce-scatter.7
  155.0 54.0 reduce-scatter.9
  213.5 60.6 reduce-scatter.5
where the time goes:
time: 282 us; the launch traced here: 281 us
  waiting for transfers between devices  187 us (66%)
  between operations  27.8 us (10%)
  matrix products  21.5 us (8%)
  starting transfers between devices  21.5 us (8%)
  local copies, waits for them, and re-layouts  11.4 us (4%)
  other arithmetic  11.1 us (4%)
    reduce_scatter x1, waiting for transfers between devices, shards(): lax.psum_scatter(stacked, 'tm', scatter_dimension=1, tiled=True)  65 us
    unnamed x4, waiting for transfers between devices  58.2 us
    reduce_scatter x1, waiting for transfers between devices, shards(): lax.psum_scatter(dec_term, 'tm', scatter_dimension=0, tiled=True)  42.8 us
    all_to_all x1, waiting for transfers between devices, shards(): lax.all_to_all(carried, 'tm', split_axis=0, concat_axis=1, tiled=True)  8.67 us
    all_to_all x1, waiting for transfers between devices, shards(): lax.all_to_all(start, 'tm', split_axis=1, concat_axis=0, tiled=True)  8.54 us
    unnamed x58, local copies, waits for them, and re-layouts  8.44 us
    unnamed x2, other arithmetic  7.66 us
    all_to_all x1, starting transfers between devices, shards(): lax.all_to_all(start, 'tm', split_axis=1, concat_axis=0, tiled=True)  7.4 us
  transfers between devices with their start and end apart: 7, of which 7 were waited for; matrix products, arithmetic and copies ran while one was open for 9% of the time, Pallas kernels for 0%

commit v1 on v0

v1 whole, which is shorter than its diff:
```python
import functools

import jax
import jax.numpy as jnp
from jax import lax
from jax.experimental import pallas as pl
from jax.experimental.pallas import tpu as pltpu
from jax.sharding import PartitionSpec as P

MESH = pl.DeviceIdType.MESH
F32 = jnp.float32
BF16 = jnp.bfloat16

PATCH, EMBED, COTAN, DECODE, SMALL, LAYER = 0, 1, 2, 3, 4, 5


def dot_nt(a, b):
    return lax.dot_general(a, b, (((1,), (1,)), ((), ())), preferred_element_type=F32)


def dot_nn(a, b):
    return jnp.dot(a, b, preferred_element_type=F32)


def step_kernel(
    n, layers, margin, chunk,
    dil, kind_row, patches, enc_w, temp_w, dec_w, cot,
    decoded, grad_enc, grad_temp, grad_dec,
    px, ct, emb, lat, slope, lat_t, px_t, dpre, car, dec_send, g_send, g_recv, s_send, s_recv,
    send_sem, recv_sem,
):
    me = lax.axis_index("tm")
    block = px.shape[1]
    tokens = n * block
    width = enc_w.shape[1]
    spans = [(c * chunk, chunk) for c in range(tokens // chunk)]

    def latents(layer, lo, size):
        first = margin + lo // block
        return lat[layer, first : first + size // block].reshape(size, width)

    def put_latents(layer, lo, value):
        first = margin + lo // block
        frames = value.shape[0] // block
        lat[layer, first : first + frames] = value.reshape(frames, block, width)

    def late_latents(layer, lo, size):
        back = margin - dil[layer] + lo // block
        return jnp.concatenate([lat[layer, back + i] for i in range(size // block)], axis=0)

    def early_dpre(layer, lo, size):
        ahead = dil[layer] + lo // block
        return jnp.concatenate([dpre[ahead + i] for i in range(size // block)], axis=0)

    def copy(kind, k, src, dst):
        return pltpu.make_async_remote_copy(
            src_ref=src,
            dst_ref=dst,
            send_sem=send_sem.at[kind, k],
            recv_sem=recv_sem.at[kind, k],
            device_id={"tm": lax.rem(me + k, n)},
            device_id_type=MESH,
        )

    def descriptor(kind, k):
        peer = lax.rem(me + k, n)
        if kind == PATCH:
            return copy(kind, k, patches.at[peer], px.at[me])
        if kind == EMBED:
            return copy(kind, k, emb.at[me], emb.at[me])
        if kind == COTAN:
            return copy(kind, k, cot.at[peer], ct.at[me])
        if kind == DECODE:
            return copy(kind, k, dec_send.at[peer], decoded.at[me])
        if kind == SMALL:
            return copy(kind, k, s_send.at[peer], s_recv.at[k])
        return copy(kind, k, g_send.at[kind - LAYER, peer], g_recv.at[kind - LAYER, k])

    def landing(kind, k):
        source = lax.rem(me + n - k, n)
        if kind == PATCH:
            return copy(kind, k, patches.at[me], px.at[source])
        if kind == EMBED:
            return copy(kind, k, emb.at[me], emb.at[source])
        if kind == COTAN:
            return copy(kind, k, cot.at[me], ct.at[source])
        if kind == DECODE:
            return copy(kind, k, dec_send.at[me], decoded.at[source])
        return descriptor(kind, k)

    def each(fn):
        lax.fori_loop(1, n, lambda k, c: (fn(k), c)[1], 0)

    def start(kind):
        each(lambda k: descriptor(kind, k).start())

    def arrive(kind):
        each(lambda k: landing(kind, k).wait_recv())

    def sent(kind):
        each(lambda k: descriptor(kind, k).wait_send())

    barrier = pltpu.get_barrier_semaphore()
    each(
        lambda k: pl.semaphore_signal(
            barrier, inc=1, device_id={"tm": lax.rem(me + k, n)}, device_id_type=MESH
        )
    )
    emb[me] = kind_row[...]
    pl.semaphore_wait(barrier, n - 1)
    start(PATCH)
    start(EMBED)

    px[me] = patches[me]
    ct[me] = cot[me]
    for layer in range(layers):
        lat[layer, 0:margin] = jnp.zeros((margin, block, width), BF16)
    dpre[n : n + margin] = jnp.zeros((margin, block, width), BF16)

    arrive(PATCH)
    arrive(EMBED)
    start(COTAN)

    for lo, size in spans:
        frames = size // block
        first = lo // block
        rows = px[first : first + frames].reshape(size, px.shape[2])
        begin = dot_nn(rows, enc_w[...]).reshape(frames, block, width)
        begin = begin + emb[first : first + frames]
        put_latents(0, lo, begin.reshape(size, width).astype(BF16))
        px_t[:, lo : lo + size] = rows.T

    for layer in range(layers):
        for lo, size in spans:
            now = latents(layer, lo, size)
            late = late_latents(layer, lo, size)
            pre = dot_nn(now, temp_w[layer, 0:width, :]) + dot_nn(late, temp_w[layer, width:, :])
            s = 0.5 + 0.5 * jnp.tanh(0.5 * pre)
            act = pre * s
            put_latents(layer + 1, lo, (now.astype(F32) + act).astype(BF16))
            slope[layer, lo : lo + size, :] = s + act * (1.0 - s)
            lat_t[layer, :, lo : lo + size] = now.T

    for lo, size in spans:
        now = latents(layers, lo, size)
        out = dot_nn(now, dec_w[...]).astype(BF16)
        dec_send[lo // block : (lo + size) // block] = out.reshape(size // block, block, out.shape[1])
        lat_t[layers, :, lo : lo + size] = now.T
    start(DECODE)
    decoded[me] = dec_send[me]
    arrive(COTAN)

    for lo, size in spans:
        rows = ct[lo // block : (lo + size) // block].reshape(size, ct.shape[2])
        car[lo : lo + size, :] = dot_nt(rows, dec_w[...]).astype(BF16)

    dec_rows = s_send.shape[1] // 2
    whole_ct = ct[...].reshape(tokens, ct.shape[2])
    dec_term = dot_nn(lat_t[layers], whole_ct).astype(BF16)
    s_send[:, 0:dec_rows, :] = dec_term.reshape(n, dec_rows, dec_term.shape[1])

    for layer in reversed(range(layers)):
        for lo, size in spans:
            product = car[lo : lo + size, :].astype(F32) * slope[layer, lo : lo + size, :]
            dpre[lo // block : (lo + size) // block] = product.astype(BF16).reshape(
                size // block, block, width
            )
        half = n // 2
        top = dot_nn(lat_t[layer], dpre[0:n].reshape(tokens, width))
        g_send[layer, 0:half] = top.astype(BF16).reshape(half, width // half, width)
        low = dot_nn(lat_t[layer], early_dpre(layer, 0, tokens))
        g_send[layer, half:n] = low.astype(BF16).reshape(half, width // half, width)
        start(LAYER + layer)
        for lo, size in spans:
            same = dpre[lo // block : (lo + size) // block].reshape(size, width)
            back = dot_nt(same, temp_w[layer, 0:width, :])
            back = back + dot_nt(early_dpre(layer, lo, size), temp_w[layer, width:, :])
            car[lo : lo + size, :] = (car[lo : lo + size, :].astype(F32) + back).astype(BF16)

    enc_term = dot_nn(px_t[...], car[...])
    enc_term = enc_term.reshape(n, enc_term.shape[0] // n, width)
    lanes = s_send.shape[2]
    enc_term = jnp.concatenate(
        [enc_term[:, :, i : i + lanes] for i in range(0, width, lanes)], axis=1
    )
    s_send[:, dec_rows:, :] = enc_term.astype(BF16)
    start(SMALL)

    for layer in reversed(range(layers)):
        arrive(LAYER + layer)
        total = g_send[layer, me].astype(F32)
        for k in range(1, n):
            total = total + g_recv[layer, k].astype(F32)
        grad_temp[layer] = total
    arrive(SMALL)
    total = s_send[me].astype(F32)
    for k in range(1, n):
        total = total + s_recv[k].astype(F32)
    grad_dec[...] = total[0:dec_rows]
    enc_rows = grad_enc.shape[0]
    for i in range(width // lanes):
        first = dec_rows + i * enc_rows
        grad_enc[:, i * lanes : (i + 1) * lanes] = total[first : first + enc_rows]
    arrive(DECODE)
    for kind in range(LAYER + layers):
        sent(kind)


def kernel_shards(
    n, patches, classes, dilations, enc_weight, cond_table, temp_weight, dec_weight, cotangent
):
    _, pixels, features = patches.shape
    layers, deep, width = temp_weight.shape
    block = pixels // n
    margin = n // 4
    tokens = n * block
    own = deep // n
    lanes = features
    small = 2 * (width // n)
    vmem = pl.BlockSpec(memory_space=pltpu.VMEM)
    smem = pl.BlockSpec(memory_space=pltpu.SMEM)
    chunk = tokens // 2
    kinds = cond_table.shape[0]
    onehot = (classes[:, None] == jnp.arange(kinds, dtype=jnp.int32)[None, :]).astype(BF16)
    kind_row = jnp.dot(onehot, cond_table, preferred_element_type=F32)
    decoded, grad_enc, grad_temp, grad_dec = pl.pallas_call(
        functools.partial(step_kernel, n, layers, margin, chunk),
        out_shape=(
            jax.ShapeDtypeStruct((n, block, features), BF16),
            jax.ShapeDtypeStruct((features // n, width), F32),
            jax.ShapeDtypeStruct((layers, own, width), F32),
            jax.ShapeDtypeStruct((width // n, features), F32),
        ),
        in_specs=[smem] + [vmem] * 6,
        out_specs=(vmem,) * 4,
        scratch_shapes=[
            pltpu.VMEM((n, block, features), BF16),
            pltpu.VMEM((n, block, features), BF16),
            pltpu.VMEM((n, 1, width), F32),
            pltpu.VMEM((layers + 1, margin + n, block, width), BF16),
            pltpu.VMEM((layers, tokens, width), F32),
            pltpu.VMEM((layers + 1, width, tokens), BF16),
            pltpu.VMEM((features, tokens), BF16),
            pltpu.VMEM((n + margin, block, width), BF16),
            pltpu.VMEM((tokens, width), BF16),
            pltpu.VMEM((n, block, features), BF16),
            pltpu.VMEM((layers, n, own, width), BF16),
            pltpu.VMEM((layers, n, own, width), BF16),
            pltpu.VMEM((n, small, lanes), BF16),
            pltpu.VMEM((n, small, lanes), BF16),
            pltpu.SemaphoreType.DMA((LAYER + layers, n)),
            pltpu.SemaphoreType.DMA((LAYER + layers, n)),
        ],
        compiler_params=pltpu.CompilerParams(
            collective_id=0, has_side_effects=True, vmem_limit_bytes=48 * 1024 * 1024
        ),
    )(
        dilations, kind_row, patches.reshape(n, block, features), enc_weight,
        temp_weight, dec_weight, cotangent.reshape(n, block, features),
    )
    return decoded.reshape(1, pixels, features), grad_enc, grad_temp, grad_dec


def shift_late(values, spacing, margin):
    filler = jnp.zeros((margin,) + values.shape[1:], values.dtype)
    padded = jnp.concatenate([filler, values], axis=0)
    return lax.dynamic_slice_in_dim(padded, margin - spacing, values.shape[0], 0)


def shift_early(values, spacing, margin):
    filler = jnp.zeros((margin,) + values.shape[1:], values.dtype)
    padded = jnp.concatenate([values, filler], axis=0)
    return lax.dynamic_slice_in_dim(padded, spacing, values.shape[0], 0)


def plain_shards(
    patches, classes, dilations, enc_weight, cond_table, temp_weight, dec_weight, cotangent
):
    layers, _, width = temp_weight.shape
    block_patches = lax.all_to_all(patches, "tm", split_axis=1, concat_axis=0, tiled=True)
    block_cot = lax.all_to_all(cotangent, "tm", split_axis=1, concat_axis=0, tiled=True)
    frame_kinds = lax.all_gather(classes, "tm", tiled=True)
    kinds = cond_table.shape[0]
    onehot = (frame_kinds[:, None] == jnp.arange(kinds, dtype=jnp.int32)[None, :]).astype(BF16)
    embedded = jnp.dot(onehot, cond_table, preferred_element_type=F32)
    begin = jnp.einsum("tpc,cd->tpd", block_patches, enc_weight, preferred_element_type=F32)
    latent = (begin + embedded[:, None, :]).astype(BF16)
    margin = latent.shape[0] // 4
    saved = []
    for layer in range(layers):
        joined = jnp.concatenate([latent, shift_late(latent, dilations[layer], margin)], axis=-1)
        pre = jnp.einsum("tpk,kd->tpd", joined, temp_weight[layer], preferred_element_type=F32)
        saved.append((joined, pre))
        latent = (latent.astype(F32) + jax.nn.silu(pre)).astype(BF16)
    block_out = jnp.einsum(
        "tpd,dc->tpc", latent, dec_weight, preferred_element_type=F32
    ).astype(BF16)
    decoded = lax.all_to_all(block_out, "tm", split_axis=0, concat_axis=1, tiled=True)
    dec_term = jnp.einsum("tpd,tpc->dc", latent, block_cot, preferred_element_type=F32)
    carried = jnp.einsum(
        "tpc,dc->tpd", block_cot, dec_weight, preferred_element_type=F32
    ).astype(BF16)
    terms = [None] * layers
    for layer in reversed(range(layers)):
        joined, pre = saved[layer]
        s = jax.nn.sigmoid(pre)
        dpre = (carried.astype(F32) * s * (1.0 + pre * (1.0 - s))).astype(BF16)
        terms[layer] = jnp.einsum("tpk,tpd->kd", joined, dpre, preferred_element_type=F32)
        back = jnp.einsum("tpd,kd->tpk", dpre, temp_weight[layer], preferred_element_type=F32)
        carried = (
            carried.astype(F32)
            + back[..., :width]
            + shift_early(back[..., width:], dilations[layer], margin)
        ).astype(BF16)
    enc_term = jnp.einsum("tpc,tpd->cd", block_patches, carried, preferred_element_type=F32)
    return (
        decoded,
        lax.psum_scatter(enc_term, "tm", scatter_dimension=0, tiled=True),
        lax.psum_scatter(jnp.stack(terms), "tm", scatter_dimension=1, tiled=True),
        lax.psum_scatter(dec_term, "tm", scatter_dimension=0, tiled=True),
    )


def solution(mesh):
    n = mesh.shape["tm"]

    def shards(patches, *rest):
        pixels = patches.shape[1]
        deep, width = rest[4].shape[1:]
        whole = pixels % n == 0 and (pixels // n) % 16 == 0 and (deep // n) % 16 == 0
        if whole and patches.shape[0] == 1 and (width // n) % 16 == 0:
            return kernel_shards(n, patches, *rest)
        return plain_shards(patches, *rest)

    in_specs = (
        P(("group", "tm"), None, None),
        P(("group", "tm")),
        P(),
        P(),
        P(),
        P(),
        P(),
        P(("group", "tm"), None, None),
    )
    out_specs = (
        P(("group", "tm"), None, None),
        P(("group", "tm"), None),
        P("group", "tm", None),
        P(("group", "tm"), None),
    )
    return jax.shard_map(shards, mesh=mesh, in_specs=in_specs, out_specs=out_specs, check_vma=False)
```

time: 282 us -> 66.7 us (0.24)
  waiting for transfers between devices: 187 us -> 0 us
  Pallas kernels: 0 us -> 57 us
  between operations: 27.8 us -> 1.31 us
  starting transfers between devices: 21.5 us -> 0 us
  matrix products: 21.5 us -> 0.12 us
  other arithmetic: 11.1 us -> 0 us
  local copies, waits for them, and re-layouts: 11.4 us -> 7.93 us
    reduce_scatter x2 -> x0, waiting for transfers between devices: 108 us -> none  [the longest x1 65 us: shards(): lax.psum_scatter(stacked, 'tm', scatter_dimension=1, tiled=True)]
    unnamed x4 -> x0, waiting for transfers between devices: 58.2 us -> none
    pallas_call x0 -> x1, Pallas kernels: none -> 57 us  [kernel_shards(): pl.pallas_call(functools.partial(step_kernel, n, layers, margin, chunk),...]
    all_to_all x4 -> x0, waiting for transfers between devices: 21.5 us -> none  [the longest x1 8.67 us: shards(): lax.all_to_all(carried, 'tm', split_axis=0, concat_axis=1, tiled=True)]
    dot_general x18 -> x1, matrix products: 21.5 us -> 0.12 us  [kernel_shards(): kind_row = jnp.dot(onehot, cond_table, preferred_element_type=F32)]
    all_to_all x4 -> x0, starting transfers between devices: 21.3 us -> none  [the longest x1 7.4 us: shards(): lax.all_to_all(start, 'tm', split_axis=1, concat_axis=0, tiled=True)]
    unnamed x2 -> x0, other arithmetic: 7.66 us -> none
    unnamed x58 -> x18, local copies, waits for them, and re-layouts: 8.44 us -> 7.93 us
  transfers between devices with their start and end apart: 7 -> 0, of which waited for: 7 -> 0; matrix products, arithmetic and copies ran while one was open for 9% -> 0% of each run, Pallas kernels for 0% -> 0%
where the time goes in v1:
time: 66.7 us; the launch traced here: 66.4 us
  Pallas kernels  57 us (85%)
  local copies, waits for them, and re-layouts  7.93 us (12%)
  between operations  1.31 us (2%)
    pallas_call x1, Pallas kernels, kernel_shards(): pl.pallas_call(functools.partial(step_kernel, n, layers, margin, chunk),...  57 us
    unnamed x18, local copies, waits for them, and re-layouts  7.93 us

profile of v1, /device:TPU:0, one launch (start us, length us, event | category | flops | bytes accessed | tf_op | source)
XLA Modules:
  0.0 66.4 jit_solution(17518622324739418134)
XLA Ops:
  0.6 0.0 copy-start
  1.3 0.0 copy-done
  1.3 0.0 copy-start.6
  1.3 0.1 fusion.kind_row
  1.5 0.5 copy-done.6
  2.0 0.0 copy-start.1
  2.0 1.2 %copy-done.1 = bf16[4,512,256]{2,1,0:T(8,128)(2,1)S(1)} copy-done((bf16[4,512,256]{2,1,0:T(8,128)(2,1)S(1)}, bf16[4,512,256]{2,1,0:T(8,128)(2,1)}, u32[]{:S(2)}) %copy-start.1) | copy-done | bytes 1048600
  3.2 0.0 copy-start.2
  3.2 0.9 %copy-done.2 = bf16[1,1024,128]{2,1,0:T(8,128)(2,1)S(1)} copy-done((bf16[1,1024,128]{2,1,0:T(8,128)(2,1)S(1)}, bf16[1,1024,128]{2,1,0:T(8,128)(2,1)}, u32[]{:S(2)}) %copy-start.2) | copy-done | bytes 262168
  4.2 0.0 copy-start.3
  4.2 0.9 %copy-done.3 = bf16[1,1024,128]{2,1,0:T(8,128)(2,1)S(1)} copy-done((bf16[1,1024,128]{2,1,0:T(8,128)(2,1)S(1)}, bf16[1,1024,128]{2,1,0:T(8,128)(2,1)}, u32[]{:S(2)}) %copy-start.3) | copy-done | bytes 262168
  5.1 0.0 copy-start.4
  5.1 0.8 %copy-done.4 = bf16[128,256]{1,0:T(8,128)(2,1)S(1)} copy-done((bf16[128,256]{1,0:T(8,128)(2,1)S(1)}, bf16[128,256]{1,0:T(8,128)(2,1)}, u32[]{:S(2)}) %copy-start.4) | copy-done | bytes 65560
  6.0 0.0 copy-start.5
  6.0 0.8 %copy-done.5 = bf16[256,128]{1,0:T(8,128)(2,1)S(1)} copy-done((bf16[256,128]{1,0:T(8,128)(2,1)S(1)}, bf16[256,128]{1,0:T(8,128)(2,1)}, u32[]{:S(2)}) %copy-start.5) | copy-done | bytes 65560
  6.8 57.0 %shard_map.111 = (bf16[16,64,128]{2,1,0:T(8,128)(2,1)S(1)}, f32[8,256]{1,0:T(8,128)S(1)}, f32[4,32,256]{2,1,0:T(8,128)S(1)}, f32[16,128]{1,0:T(8,128)S(1)}) custom-call(s32[4]{0:T(128)S(1)} %copy-done.6, f32[1,256]{1,0:T(1,128)S(1)} %fusion.kind_row, bf16[16,64,128]{2,1,0:T(8,128)(2,1)S(1)} %bitcast.11, bf16[128,256]{1,0:T(8,128)(2,1)S(1)} %copy-done.4, ...), custom_call_target="tpu_custom_call" | custom-call | tf_op jit(solution)/shard_map/pallas_call | solution.py:226
  63.8 0.7 %copy.17 = bf16[1,1024,128]{2,1,0:T(8,128)(2,1)} copy(bf16[1,1024,128]{2,1,0:T(8,128)(2,1)S(1)} %bitcast.10) | data formatting | bytes 524288
  64.5 0.6 copy.18
  65.1 0.7 copy.19
  65.8 0.6 copy.20
Async XLA Ops:
  0.6 0.7 %copy-start = (bf16[16,256]{1,0:T(8,128)(2,1)S(1)}, bf16[16,256]{1,0:T(8,128)(2,1)}, u32[]{:S(2)}) copy-start(bf16[16,256]{1,0:T(8,128)(2,1)} %param.12) | copy-start | bytes 24580
  1.3 0.7 copy-start.6
  2.0 1.2 %copy-start.1 = (bf16[4,512,256]{2,1,0:T(8,128)(2,1)S(1)}, bf16[4,512,256]{2,1,0:T(8,128)(2,1)}, u32[]{:S(2)}) copy-start(bf16[4,512,256]{2,1,0:T(8,128)(2,1)} %temp_w.1) | copy-start | bytes 3145732
  3.2 0.9 %copy-start.2 = (bf16[1,1024,128]{2,1,0:T(8,128)(2,1)S(1)}, bf16[1,1024,128]{2,1,0:T(8,128)(2,1)}, u32[]{:S(2)}) copy-start(bf16[1,1024,128]{2,1,0:T(8,128)(2,1)} %param.8) | copy-start | bytes 786436
  4.2 0.9 %copy-start.3 = (bf16[1,1024,128]{2,1,0:T(8,128)(2,1)S(1)}, bf16[1,1024,128]{2,1,0:T(8,128)(2,1)}, u32[]{:S(2)}) copy-start(bf16[1,1024,128]{2,1,0:T(8,128)(2,1)} %param.15) | copy-start | bytes 786436
  5.1 0.8 %copy-start.4 = (bf16[128,256]{1,0:T(8,128)(2,1)S(1)}, bf16[128,256]{1,0:T(8,128)(2,1)}, u32[]{:S(2)}) copy-start(bf16[128,256]{1,0:T(8,128)(2,1)} %enc_w.1) | copy-start | bytes 196612
  6.0 0.8 %copy-start.5 = (bf16[256,128]{1,0:T(8,128)(2,1)S(1)}, bf16[256,128]{1,0:T(8,128)(2,1)}, u32[]{:S(2)}) copy-start(bf16[256,128]{1,0:T(8,128)(2,1)} %dec_w.1) | copy-start | bytes 196612

commit v2 on v1

--- a/solution.py
+++ b/solution.py
@@ -11,7 +11,7 @@
 F32 = jnp.float32
 BF16 = jnp.bfloat16
 
-PATCH, EMBED, COTAN, DECODE, SMALL, LAYER = 0, 1, 2, 3, 4, 5
+PATCH, EMBED, COTAN, DECODE, DEC_TERM, ENC_TERM = range(6)
 
 
 def dot_nt(a, b):
@@ -24,33 +24,38 @@
 
 def step_kernel(
     n, layers, margin, chunk,
-    dil, kind_row, patches, enc_w, temp_w, dec_w, cot,
+    dil, cls, patches, enc_hbm, cond_hbm, temp_hbm, dec_hbm, cot,
     decoded, grad_enc, grad_temp, grad_dec,
-    px, ct, emb, lat, slope, lat_t, px_t, dpre, car, dec_send, g_send, g_recv, s_send, s_recv,
-    send_sem, recv_sem,
+    enc_w, cond, temp_w, dec_w, cond_rows,
+    px, ct, emb, lat, slope, lat_t, px_t, dpre, car, dec_send,
+    core_out, core_in, y_out, y_in, z_out, z_in, d_out, d_in, e_out, e_in,
+    local_sem, send_sem, recv_sem, stage_send, stage_recv,
 ):
     me = lax.axis_index("tm")
+    core = lax.rem(me, 2)
+    y = lax.rem(lax.div(me, 2), 2)
+    z = lax.div(me, 4)
+    nz = n // 4
     block = px.shape[1]
     tokens = n * block
     width = enc_w.shape[1]
-    spans = [(c * chunk, chunk) for c in range(tokens // chunk)]
-
-    def latents(layer, lo, size):
-        first = margin + lo // block
-        return lat[layer, first : first + size // block].reshape(size, width)
-
-    def put_latents(layer, lo, value):
-        first = margin + lo // block
-        frames = value.shape[0] // block
-        lat[layer, first : first + frames] = value.reshape(frames, block, width)
-
-    def late_latents(layer, lo, size):
-        back = margin - dil[layer] + lo // block
-        return jnp.concatenate([lat[layer, back + i] for i in range(size // block)], axis=0)
-
-    def early_dpre(layer, lo, size):
-        ahead = dil[layer] + lo // block
-        return jnp.concatenate([dpre[ahead + i] for i in range(size // block)], axis=0)
+    own = core_out.shape[4]
+
+    local = [
+        pltpu.make_async_copy(src, dst, local_sem.at[i])
+        for i, (src, dst) in enumerate(
+            [
+                (cond_hbm, cond),
+                (patches.at[me], px.at[me]),
+                (enc_hbm, enc_w),
+                (temp_hbm, temp_w),
+                (dec_hbm, dec_w),
+                (cot.at[me], ct.at[me]),
+            ]
+        )
+    ]
+    for fetch in local:
+        fetch.start()
 
     def copy(kind, k, src, dst):
         return pltpu.make_async_remote_copy(
@@ -72,9 +77,9 @@
             return copy(kind, k, cot.at[peer], ct.at[me])
         if kind == DECODE:
             return copy(kind, k, dec_send.at[peer], decoded.at[me])
-        if kind == SMALL:
-            return copy(kind, k, s_send.at[peer], s_recv.at[k])
-        return copy(kind, k, g_send.at[kind - LAYER, peer], g_recv.at[kind - LAYER, k])
+        if kind == DEC_TERM:
+            return copy(kind, k, d_out.at[peer], d_in.at[k])
+        return copy(kind, k, e_out.at[peer], e_in.at[k])
 
     def landing(kind, k):
         source = lax.rem(me + n - k, n)
@@ -100,26 +105,98 @@
     def sent(kind):
         each(lambda k: descriptor(kind, k).wait_send())
 
+    def staged(layer, stage, src, dst, peer):
+        return pltpu.make_async_remote_copy(
+            src_ref=src,
+            dst_ref=dst,
+            send_sem=stage_send.at[layer, stage],
+            recv_sem=stage_recv.at[layer, stage],
+            device_id={"tm": peer},
+            device_id_type=MESH,
+        )
+
+    def core_copy(layer):
+        return staged(
+            layer, 0, core_out.at[layer, 1 - core], core_in.at[layer], me + 1 - 2 * core
+        )
+
+    def y_copy(layer):
+        return staged(layer, 1, y_out.at[layer], y_in.at[layer], me + 2 - 4 * y)
+
+    def z_copy(layer, k):
+        there = lax.rem(z + k, nz)
+        peer = there * 4 + y * 2 + core
+        return staged(layer, 1 + k, z_out.at[layer, there], z_in.at[layer, k], peer)
+
+    def send_core(layer):
+        core_copy(layer).start()
+
+    def send_y(layer):
+        core_copy(layer).wait_recv()
+        total = core_out[layer, core, 1 - y].astype(F32) + core_in[layer, 1 - y].astype(F32)
+        y_out[layer] = total.astype(BF16)
+        y_copy(layer).start()
+
+    def send_z(layer):
+        y_copy(layer).wait_recv()
+        total = core_out[layer, core, y].astype(F32) + core_in[layer, y].astype(F32)
+        z_out[layer] = (total + y_in[layer].astype(F32)).astype(BF16)
+        for k in range(1, nz):
+            z_copy(layer, k).start()
+
+    def finish(layer):
+        total = z_out[layer, z].astype(F32)
+        for k in range(1, nz):
+            z_copy(layer, k).wait_recv()
+            total = total + z_in[layer, k].astype(F32)
+        grad_temp[layer] = total
+        core_copy(layer).wait_send()
+        y_copy(layer).wait_send()
+        for k in range(1, nz):
+            z_copy(layer, k).wait_send()
+
     barrier = pltpu.get_barrier_semaphore()
     each(
         lambda k: pl.semaphore_signal(
             barrier, inc=1, device_id={"tm": lax.rem(me + k, n)}, device_id_type=MESH
         )
     )
-    emb[me] = kind_row[...]
     pl.semaphore_wait(barrier, n - 1)
     start(PATCH)
+    local[0].wait()
+    kinds = cond.shape[0]
+    cond_rows[...] = cond[...].astype(F32).reshape(kinds, 1, width)
+    emb[me] = cond_rows[cls[0]]
     start(EMBED)
 
-    px[me] = patches[me]
-    ct[me] = cot[me]
+    spans = [(c * chunk, chunk) for c in range(tokens // chunk)]
+
+    def latents(layer, lo, size):
+        first = margin + lo // block
+        return lat[layer, first : first + size // block].reshape(size, width)
+
+    def put_latents(layer, lo, value):
+        first = margin + lo // block
+        frames = value.shape[0] // block
+        lat[layer, first : first + frames] = value.reshape(frames, block, width)
+
+    def late_latents(layer, lo, size):
+        back = margin - dil[layer] + lo // block
+        return jnp.concatenate([lat[layer, back + i] for i in range(size // block)], axis=0)
+
+    def early_dpre(layer, lo, size):
+        ahead = dil[layer] + lo // block
+        return jnp.concatenate([dpre[ahead + i] for i in range(size // block)], axis=0)
+
     for layer in range(layers):
         lat[layer, 0:margin] = jnp.zeros((margin, block, width), BF16)
     dpre[n : n + margin] = jnp.zeros((margin, block, width), BF16)
 
+    for fetch in local[1:]:
+        fetch.wait()
     arrive(PATCH)
+    start(COTAN)
     arrive(EMBED)
-    start(COTAN)
 
     for lo, size in spans:
         frames = size // block
@@ -154,56 +231,66 @@
         rows = ct[lo // block : (lo + size) // block].reshape(size, ct.shape[2])
         car[lo : lo + size, :] = dot_nt(rows, dec_w[...]).astype(BF16)
 
-    dec_rows = s_send.shape[1] // 2
+    dec_rows = d_out.shape[1]
     whole_ct = ct[...].reshape(tokens, ct.shape[2])
     dec_term = dot_nn(lat_t[layers], whole_ct).astype(BF16)
-    s_send[:, 0:dec_rows, :] = dec_term.reshape(n, dec_rows, dec_term.shape[1])
-
+    d_out[...] = dec_term.reshape(n, dec_rows, dec_term.shape[1])
+    start(DEC_TERM)
+
+    half = n // 2
     for layer in reversed(range(layers)):
         for lo, size in spans:
             product = car[lo : lo + size, :].astype(F32) * slope[layer, lo : lo + size, :]
             dpre[lo // block : (lo + size) // block] = product.astype(BF16).reshape(
                 size // block, block, width
             )
-        half = n // 2
-        top = dot_nn(lat_t[layer], dpre[0:n].reshape(tokens, width))
-        g_send[layer, 0:half] = top.astype(BF16).reshape(half, width // half, width)
-        low = dot_nn(lat_t[layer], early_dpre(layer, 0, tokens))
-        g_send[layer, half:n] = low.astype(BF16).reshape(half, width // half, width)
-        start(LAYER + layer)
+        top = dot_nn(lat_t[layer], dpre[0:n].reshape(tokens, width)).astype(BF16)
+        low = dot_nn(lat_t[layer], early_dpre(layer, 0, tokens)).astype(BF16)
+        for j in range(n):
+            piece = top if j < half else low
+            first = (j % half) * own
+            core_out[layer, j % 2, (j // 2) % 2, j // 4] = piece[first : first + own]
+        send_core(layer)
+        if layer + 1 < layers:
+            send_y(layer + 1)
+        if layer + 2 < layers:
+            send_z(layer + 2)
         for lo, size in spans:
             same = dpre[lo // block : (lo + size) // block].reshape(size, width)
             back = dot_nt(same, temp_w[layer, 0:width, :])
             back = back + dot_nt(early_dpre(layer, lo, size), temp_w[layer, width:, :])
             car[lo : lo + size, :] = (car[lo : lo + size, :].astype(F32) + back).astype(BF16)
+    send_y(0)
+    send_z(1)
 
     enc_term = dot_nn(px_t[...], car[...])
     enc_term = enc_term.reshape(n, enc_term.shape[0] // n, width)
-    lanes = s_send.shape[2]
+    lanes = e_out.shape[2]
     enc_term = jnp.concatenate(
         [enc_term[:, :, i : i + lanes] for i in range(0, width, lanes)], axis=1
     )
-    s_send[:, dec_rows:, :] = enc_term.astype(BF16)
-    start(SMALL)
-
-    for layer in reversed(range(layers)):
-        arrive(LAYER + layer)
-        total = g_send[layer, me].astype(F32)
-        for k in range(1, n):
-            total = total + g_recv[layer, k].astype(F32)
-        grad_temp[layer] = total
-    arrive(SMALL)
-    total = s_send[me].astype(F32)
+    e_out[...] = enc_term.astype(BF16)
+    start(ENC_TERM)
+    send_z(0)
+
+    arrive(DEC_TERM)
+    total = d_out[me].astype(F32)
     for k in range(1, n):
-        total = total + s_recv[k].astype(F32)
-    grad_dec[...] = total[0:dec_rows]
+        total = total + d_in[k].astype(F32)
+    grad_dec[...] = total
+    for layer in range(layers - 1, 0, -1):
+        finish(layer)
+    arrive(DECODE)
+    arrive(ENC_TERM)
+    total = e_out[me].astype(F32)
+    for k in range(1, n):
+        total = total + e_in[k].astype(F32)
     enc_rows = grad_enc.shape[0]
     for i in range(width // lanes):
-        first = dec_rows + i * enc_rows
-        grad_enc[:, i * lanes : (i + 1) * lanes] = total[first : first + enc_rows]
-    arrive(DECODE)
-    for kind in range(LAYER + layers):
+        grad_enc[:, i * lanes : (i + 1) * lanes] = total[i * enc_rows : (i + 1) * enc_rows]
+    for kind in range(ENC_TERM + 1):
         sent(kind)
+    finish(0)
 
 
 def kernel_shards(
@@ -216,13 +303,13 @@
     tokens = n * block
     own = deep // n
     lanes = features
-    small = 2 * (width // n)
+    nz = n // 4
+    hbm = pl.BlockSpec(memory_space=pltpu.HBM)
+    kinds = cond_table.shape[0]
+    small = width // n
     vmem = pl.BlockSpec(memory_space=pltpu.VMEM)
     smem = pl.BlockSpec(memory_space=pltpu.SMEM)
     chunk = tokens // 2
-    kinds = cond_table.shape[0]
-    onehot = (classes[:, None] == jnp.arange(kinds, dtype=jnp.int32)[None, :]).astype(BF16)
-    kind_row = jnp.dot(onehot, cond_table, preferred_element_type=F32)
     decoded, grad_enc, grad_temp, grad_dec = pl.pallas_call(
         functools.partial(step_kernel, n, layers, margin, chunk),
         out_shape=(
@@ -231,9 +318,14 @@
             jax.ShapeDtypeStruct((layers, own, width), F32),
             jax.ShapeDtypeStruct((width // n, features), F32),
         ),
-        in_specs=[smem] + [vmem] * 6,
+        in_specs=[smem, smem] + [hbm] * 6,
         out_specs=(vmem,) * 4,
         scratch_shapes=[
+            pltpu.VMEM((features, width), BF16),
+            pltpu.VMEM((kinds, width), BF16),
+            pltpu.VMEM((layers, deep, width), BF16),
+            pltpu.VMEM((width, features), BF16),
+            pltpu.VMEM((kinds, 1, width), F32),
             pltpu.VMEM((n, block, features), BF16),
             pltpu.VMEM((n, block, features), BF16),
             pltpu.VMEM((n, 1, width), F32),
@@ -244,18 +336,27 @@
             pltpu.VMEM((n + margin, block, width), BF16),
             pltpu.VMEM((tokens, width), BF16),
             pltpu.VMEM((n, block, features), BF16),
-            pltpu.VMEM((layers, n, own, width), BF16),
-            pltpu.VMEM((layers, n, own, width), BF16),
+            pltpu.VMEM((layers, 2, 2, nz, own, width), BF16),
+            pltpu.VMEM((layers, 2, nz, own, width), BF16),
+            pltpu.VMEM((layers, nz, own, width), BF16),
+            pltpu.VMEM((layers, nz, own, width), BF16),
+            pltpu.VMEM((layers, nz, own, width), BF16),
+            pltpu.VMEM((layers, nz, own, width), BF16),
             pltpu.VMEM((n, small, lanes), BF16),
             pltpu.VMEM((n, small, lanes), BF16),
-            pltpu.SemaphoreType.DMA((LAYER + layers, n)),
-            pltpu.SemaphoreType.DMA((LAYER + layers, n)),
+            pltpu.VMEM((n, small, lanes), BF16),
+            pltpu.VMEM((n, small, lanes), BF16),
+            pltpu.SemaphoreType.DMA((6,)),
+            pltpu.SemaphoreType.DMA((ENC_TERM + 1, n)),
+            pltpu.SemaphoreType.DMA((ENC_TERM + 1, n)),
+            pltpu.SemaphoreType.DMA((layers, nz + 1)),
+            pltpu.SemaphoreType.DMA((layers, nz + 1)),
         ],
         compiler_params=pltpu.CompilerParams(
             collective_id=0, has_side_effects=True, vmem_limit_bytes=48 * 1024 * 1024
         ),
     )(
-        dilations, kind_row, patches.reshape(n, block, features), enc_weight,
+        dilations, classes, patches.reshape(n, block, features), enc_weight, cond_table,
         temp_weight, dec_weight, cotangent.reshape(n, block, features),
     )
     return decoded.reshape(1, pixels, features), grad_enc, grad_temp, grad_dec
@@ -327,7 +428,7 @@
     def shards(patches, *rest):
         pixels = patches.shape[1]
         deep, width = rest[4].shape[1:]
-        whole = pixels % n == 0 and (pixels // n) % 16 == 0 and (deep // n) % 16 == 0
+        whole = n % 4 == 0 and n >= 8 and pixels % n == 0 and (pixels // n) % 16 == 0 and (deep // n) % 16 == 0
         if whole and patches.shape[0] == 1 and (width // n) % 16 == 0:
             return kernel_shards(n, patches, *rest)
         return plain_shards(patches, *rest)

time: 66.7 us -> 51.8 us (0.78)
  Pallas kernels: 57 us -> 41.5 us
  local copies, waits for them, and re-layouts: 7.93 us -> 8.7 us
    pallas_call x1, Pallas kernels: 57 us -> 41.5 us  [kernel_shards(): pl.pallas_call(functools.partial(step_kernel, n, layers, margin, chunk),...]
    unnamed x18, local copies, waits for them, and re-layouts: 7.93 us -> 8.7 us
where the time goes in v2:
time: 51.8 us; the launch traced here: 51.5 us
  Pallas kernels  41.5 us (80%)
  local copies, waits for them, and re-layouts  8.7 us (17%)
  between operations  1.3 us (3%)
    pallas_call x1, Pallas kernels, kernel_shards(): pl.pallas_call(functools.partial(step_kernel, n, layers, margin, chunk),...  41.5 us
    unnamed x18, local copies, waits for them, and re-layouts  8.7 us

profile of v2, /device:TPU:0, one launch (start us, length us, event | category | flops | bytes accessed | tf_op | source)
XLA Modules:
  0.0 51.5 jit_solution(15569697724277877026)
XLA Ops:
  1.3 0.0 copy-start.6
  1.3 0.6 %copy-done.6 = s32[4]{0:T(128)S(1)} copy-done((s32[4]{0:T(128)S(1)}, s32[4]{0:T(128)}, u32[]{:S(2)}) %copy-start.6) | copy-done | bytes 40
  1.9 0.0 copy-start
  1.9 1.2 %copy-done = bf16[4,512,256]{2,1,0:T(8,128)(2,1)S(1)} copy-done((bf16[4,512,256]{2,1,0:T(8,128)(2,1)S(1)}, bf16[4,512,256]{2,1,0:T(8,128)(2,1)}, u32[]{:S(2)}) %copy-start) | copy-done | bytes 1048600
  3.2 0.0 copy-start.1
  3.2 0.9 %copy-done.1 = bf16[1,1024,128]{2,1,0:T(8,128)(2,1)S(1)} copy-done((bf16[1,1024,128]{2,1,0:T(8,128)(2,1)S(1)}, bf16[1,1024,128]{2,1,0:T(8,128)(2,1)}, u32[]{:S(2)}) %copy-start.1) | copy-done | bytes 262168
  4.1 0.0 copy-start.2
  4.1 0.9 %copy-done.2 = bf16[1,1024,128]{2,1,0:T(8,128)(2,1)S(1)} copy-done((bf16[1,1024,128]{2,1,0:T(8,128)(2,1)S(1)}, bf16[1,1024,128]{2,1,0:T(8,128)(2,1)}, u32[]{:S(2)}) %copy-start.2) | copy-done | bytes 262168
  5.1 0.0 copy-start.3
  5.1 0.8 %copy-done.3 = bf16[128,256]{1,0:T(8,128)(2,1)S(1)} copy-done((bf16[128,256]{1,0:T(8,128)(2,1)S(1)}, bf16[128,256]{1,0:T(8,128)(2,1)}, u32[]{:S(2)}) %copy-start.3) | copy-done | bytes 65560
  5.9 0.0 copy-start.4
  5.9 0.8 %copy-done.4 = bf16[256,128]{1,0:T(8,128)(2,1)S(1)} copy-done((bf16[256,128]{1,0:T(8,128)(2,1)S(1)}, bf16[256,128]{1,0:T(8,128)(2,1)}, u32[]{:S(2)}) %copy-start.4) | copy-done | bytes 65560
  6.7 0.0 copy-start.5
  6.7 0.7 %copy-done.5 = bf16[16,256]{1,0:T(8,128)(2,1)S(1)} copy-done((bf16[16,256]{1,0:T(8,128)(2,1)S(1)}, bf16[16,256]{1,0:T(8,128)(2,1)}, u32[]{:S(2)}) %copy-start.5) | copy-done | bytes 8216
  7.4 41.5 %shard_map.111 = (bf16[16,64,128]{2,1,0:T(8,128)(2,1)S(1)}, f32[8,256]{1,0:T(8,128)S(1)}, f32[4,32,256]{2,1,0:T(8,128)S(1)}, f32[16,128]{1,0:T(8,128)S(1)}) custom-call(s32[4]{0:T(128)S(1)} %copy-done.6, s32[1]{0:T(128)S(6)} %copy.16.cls, bf16[16,64,128]{2,1,0:T(8,128)(2,1)S(1)} %bitcast.4, bf16[128,256]{1,0:T(8,128)(2,1)S(1)} %copy-done.3, ...), custom_call_target="tpu_custom_call" | custom-call | tf_op jit(solution)/shard_map/pallas_call | solution.py:313
  48.9 0.7 %copy.17 = bf16[1,1024,128]{2,1,0:T(8,128)(2,1)} copy(bf16[1,1024,128]{2,1,0:T(8,128)(2,1)S(1)} %bitcast.3) | data formatting | bytes 524288
  49.6 0.6 %copy.18 = f32[8,256]{1,0:T(8,128)} copy(f32[8,256]{1,0:T(8,128)S(1)} %get-tuple-element.17) | data formatting | bytes 16384
  50.2 0.7 %copy.19 = f32[4,32,256]{2,1,0:T(8,128)} copy(f32[4,32,256]{2,1,0:T(8,128)S(1)} %get-tuple-element.18) | data formatting | bytes 262144
  50.9 0.6 %copy.20 = f32[16,128]{1,0:T(8,128)} copy(f32[16,128]{1,0:T(8,128)S(1)} %get-tuple-element.19) | data formatting | bytes 16384
Async XLA Ops:
  1.3 0.7 %copy-start.6 = (s32[4]{0:T(128)S(1)}, s32[4]{0:T(128)}, u32[]{:S(2)}) copy-start(s32[4]{0:T(128)} %dil.1) | copy-start | bytes 52
  1.9 1.2 %copy-start = (bf16[4,512,256]{2,1,0:T(8,128)(2,1)S(1)}, bf16[4,512,256]{2,1,0:T(8,128)(2,1)}, u32[]{:S(2)}) copy-start(bf16[4,512,256]{2,1,0:T(8,128)(2,1)} %temp_hbm.1) | copy-start | bytes 3145732
  3.2 0.9 %copy-start.1 = (bf16[1,1024,128]{2,1,0:T(8,128)(2,1)S(1)}, bf16[1,1024,128]{2,1,0:T(8,128)(2,1)}, u32[]{:S(2)}) copy-start(bf16[1,1024,128]{2,1,0:T(8,128)(2,1)} %param.8) | copy-start | bytes 786436
  4.1 0.9 %copy-start.2 = (bf16[1,1024,128]{2,1,0:T(8,128)(2,1)S(1)}, bf16[1,1024,128]{2,1,0:T(8,128)(2,1)}, u32[]{:S(2)}) copy-start(bf16[1,1024,128]{2,1,0:T(8,128)(2,1)} %param.15) | copy-start | bytes 786436
  5.1 0.8 %copy-start.3 = (bf16[128,256]{1,0:T(8,128)(2,1)S(1)}, bf16[128,256]{1,0:T(8,128)(2,1)}, u32[]{:S(2)}) copy-start(bf16[128,256]{1,0:T(8,128)(2,1)} %enc_hbm.1) | copy-start | bytes 196612
  5.9 0.8 %copy-start.4 = (bf16[256,128]{1,0:T(8,128)(2,1)S(1)}, bf16[256,128]{1,0:T(8,128)(2,1)}, u32[]{:S(2)}) copy-start(bf16[256,128]{1,0:T(8,128)(2,1)} %dec_hbm.1) | copy-start | bytes 196612
  6.7 0.7 %copy-start.5 = (bf16[16,256]{1,0:T(8,128)(2,1)S(1)}, bf16[16,256]{1,0:T(8,128)(2,1)}, u32[]{:S(2)}) copy-start(bf16[16,256]{1,0:T(8,128)(2,1)} %cond_hbm.1) | copy-start | bytes 24580

commit v3 on v2

--- a/solution.py
+++ b/solution.py
@@ -61,8 +61,8 @@
         return pltpu.make_async_remote_copy(
             src_ref=src,
             dst_ref=dst,
-            send_sem=send_sem.at[kind, k],
-            recv_sem=recv_sem.at[kind, k],
+            send_sem=send_sem.at[kind],
+            recv_sem=recv_sem.at[kind],
             device_id={"tm": lax.rem(me + k, n)},
             device_id_type=MESH,
         )
@@ -81,17 +81,9 @@
             return copy(kind, k, d_out.at[peer], d_in.at[k])
         return copy(kind, k, e_out.at[peer], e_in.at[k])
 
-    def landing(kind, k):
-        source = lax.rem(me + n - k, n)
-        if kind == PATCH:
-            return copy(kind, k, patches.at[me], px.at[source])
-        if kind == EMBED:
-            return copy(kind, k, emb.at[me], emb.at[source])
-        if kind == COTAN:
-            return copy(kind, k, cot.at[me], ct.at[source])
-        if kind == DECODE:
-            return copy(kind, k, dec_send.at[me], decoded.at[source])
-        return descriptor(kind, k)
+    def everything(kind):
+        landed = [px, emb, ct, decoded, d_in, e_in][kind].at[pl.ds(1, n - 1)]
+        return copy(kind, 1, landed, landed)
 
     def each(fn):
         lax.fori_loop(1, n, lambda k, c: (fn(k), c)[1], 0)
@@ -100,10 +92,10 @@
         each(lambda k: descriptor(kind, k).start())
 
     def arrive(kind):
-        each(lambda k: landing(kind, k).wait_recv())
+        everything(kind).wait_recv()
 
     def sent(kind):
-        each(lambda k: descriptor(kind, k).wait_send())
+        everything(kind).wait_send()
 
     def staged(layer, stage, src, dst, peer):
         return pltpu.make_async_remote_copy(
@@ -161,13 +153,14 @@
             barrier, inc=1, device_id={"tm": lax.rem(me + k, n)}, device_id_type=MESH
         )
     )
-    pl.semaphore_wait(barrier, n - 1)
-    start(PATCH)
     local[0].wait()
     kinds = cond.shape[0]
     cond_rows[...] = cond[...].astype(F32).reshape(kinds, 1, width)
     emb[me] = cond_rows[cls[0]]
+    pl.semaphore_wait(barrier, n - 1)
     start(EMBED)
+    start(PATCH)
+    start(COTAN)
 
     spans = [(c * chunk, chunk) for c in range(tokens // chunk)]
 
@@ -195,7 +188,6 @@
     for fetch in local[1:]:
         fetch.wait()
     arrive(PATCH)
-    start(COTAN)
     arrive(EMBED)
 
     for lo, size in spans:
@@ -347,13 +339,13 @@
             pltpu.VMEM((n, small, lanes), BF16),
             pltpu.VMEM((n, small, lanes), BF16),
             pltpu.SemaphoreType.DMA((6,)),
-            pltpu.SemaphoreType.DMA((ENC_TERM + 1, n)),
-            pltpu.SemaphoreType.DMA((ENC_TERM + 1, n)),
+            pltpu.SemaphoreType.DMA((ENC_TERM + 1,)),
+            pltpu.SemaphoreType.DMA((ENC_TERM + 1,)),
             pltpu.SemaphoreType.DMA((layers, nz + 1)),
             pltpu.SemaphoreType.DMA((layers, nz + 1)),
         ],
         compiler_params=pltpu.CompilerParams(
-            collective_id=0, has_side_effects=True, vmem_limit_bytes=48 * 1024 * 1024
+            collective_id=0, has_side_effects=True, vmem_limit_bytes=60 * 1024 * 1024
         ),
     )(
         dilations, classes, patches.reshape(n, block, features), enc_weight, cond_table,

time: 51.8 us -> 43.6 us (0.84)
  local copies, waits for them, and re-layouts: 8.7 us -> 3.61 us
  Pallas kernels: 41.5 us -> 38.4 us
    unnamed x18 -> x10, local copies, waits for them, and re-layouts: 8.7 us -> 3.61 us
    pallas_call x1, Pallas kernels: 41.5 us -> 38.4 us  [kernel_shards(): pl.pallas_call(functools.partial(step_kernel, n, layers, margin, chunk),...]
where the time goes in v3:
time: 43.6 us; the launch traced here: 43.3 us
  Pallas kernels  38.4 us (88%)
  local copies, waits for them, and re-layouts  3.61 us (8%)
  between operations  1.31 us (3%)
    pallas_call x1, Pallas kernels, kernel_shards(): pl.pallas_call(functools.partial(step_kernel, n, layers, margin, chunk),...  38.4 us
    unnamed x10, local copies, waits for them, and re-layouts  3.61 us

profile of v3, /device:TPU:0, one launch (start us, length us, event | category | flops | bytes accessed | tf_op | source)
XLA Modules:
  0.0 43.3 jit_solution(15119042487219581601)
XLA Ops:
  1.3 38.4 %shard_map.111 = (bf16[16,64,128]{2,1,0:T(8,128)(2,1)}, f32[8,256]{1,0:T(8,128)}, f32[4,32,256]{2,1,0:T(8,128)}, f32[16,128]{1,0:T(8,128)}) custom-call(s32[4]{0:T(128)} %dil.1, s32[1]{0:T(128)S(6)} %copy.16.cls, bf16[16,64,128]{2,1,0:T(8,128)(2,1)} %bitcast.4, bf16[128,256]{1,0:T(8,128)(2,1)} %enc_hbm.1, bf16[16,256]{1,0:T(8,128)(2,1)} %cond_hbm.1, ...), custom_call_target="tpu_custom_call" | custom-call | tf_op jit(solution)/shard_map/pallas_call | solution.py:305
  39.7 0.0 copy-start.2
  39.7 0.0 copy-start
  39.7 1.7 %copy.17 = bf16[1,1024,128]{2,1,0:T(8,128)(2,1)} copy(bf16[1,1024,128]{2,1,0:T(8,128)(2,1)} %bitcast.3) | data formatting | bytes 524288
  41.4 0.0 copy-done.2
  41.4 0.6 %copy.18 = f32[8,256]{1,0:T(8,128)} copy(f32[8,256]{1,0:T(8,128)S(1)} %copy-done.2) | data formatting | bytes 16384
  42.0 0.0 copy-done
  42.0 0.0 copy-start.1
  42.0 0.7 %copy.19 = f32[4,32,256]{2,1,0:T(8,128)} copy(f32[4,32,256]{2,1,0:T(8,128)S(1)} %copy-done) | data formatting | bytes 262144
  42.7 0.0 copy-done.1
  42.7 0.6 %copy.20 = f32[16,128]{1,0:T(8,128)} copy(f32[16,128]{1,0:T(8,128)S(1)} %copy-done.1) | data formatting | bytes 16384
Async XLA Ops:
  39.7 1.7 %copy-start.2 = (f32[8,256]{1,0:T(8,128)S(1)}, f32[8,256]{1,0:T(8,128)}, u32[]{:S(2)}) copy-start(f32[8,256]{1,0:T(8,128)} %get-tuple-element.17) | copy-start | bytes 24580
  39.7 2.3 %copy-start = (f32[4,32,256]{2,1,0:T(8,128)S(1)}, f32[4,32,256]{2,1,0:T(8,128)}, u32[]{:S(2)}) copy-start(f32[4,32,256]{2,1,0:T(8,128)} %get-tuple-element.18) | copy-start | bytes 393220
  42.0 0.7 %copy-start.1 = (f32[16,128]{1,0:T(8,128)S(1)}, f32[16,128]{1,0:T(8,128)}, u32[]{:S(2)}) copy-start(f32[16,128]{1,0:T(8,128)} %get-tuple-element.19) | copy-start | bytes 24580
